TPU v7x, 32 devices: a whole 2x2x4 slice. The times are simulated.
32 devices in a mesh: dp: 16 (over z, x, core), expert: 2 (over y).
Axes of the slice: x: 2, y: 2, z: 4, core: 2. Of those that a mesh axis runs over, the one named last changes fastest.
Arguments:
- tokens: bfloat16 [2048, 2048], P('dp'), may hold values from -6 to 6
- routes: int32 [2048, 8], P('dp'), may hold values from 0 to 15, all different within a row; in each aligned block of 128 rows (0 to 127, 128 to 255, ...) at most 64 rows name the same one
- kept_mask: int32 [2048, 8], P('dp'), may hold values from 0 to 1, as said below
- gate_probs: float32 [2048, 8], P('dp'), may hold values from 0.05 to 0.5
- output_grad: bfloat16 [2048, 2048], P('dp'), may hold values from -96 to 96
- w_gate: bfloat16 [16, 2048, 1024], P('dp', None, 'expert'), may hold values from -0.125 to 0.125
- w_up: bfloat16 [16, 2048, 1024], P('dp', None, 'expert'), may hold values from -0.125 to 0.125
- w_down: bfloat16 [16, 1024, 2048], P('dp', 'expert'), may hold values from -0.1875 to 0.1875
Outputs:
- output: bfloat16 [2048, 2048], P('dp', 'expert')
- input_grad: bfloat16 [2048, 2048], P('dp', 'expert')
- grad_gate: bfloat16 [16, 2048, 1024], P('dp', None, 'expert')
- grad_up: bfloat16 [16, 2048, 1024], P('dp', None, 'expert')
- grad_down: bfloat16 [16, 1024, 2048], P('dp', 'expert')
Inputs may be any that keep to these rules, and one draw needn't show every extreme that they name: `routes`: each row names 8 different experts, and the 128 rows of each index of dp name every expert exactly 64 times. `kept_mask`: the share of kept entries varies along the tokens.
All inputs are finite; a program needn't handle non-finite values.
Results may differ from a plain program's by a relative error of at most 0.0064.
Values may be sent and summed in bfloat16 or wider, within the bound.
No kernel may reach another device: no remote copies, remote signals or barrier semaphores. Data moves between devices by JAX's collectives and lax.ppermute only.
A program may use at most 128 MiB of HBM per device.

v0:
```python
import functools
import math

import jax
import jax.numpy as jnp
from jax import lax
from jax.experimental import pallas as pl
from jax.experimental.pallas import tpu as pltpu
from jax.sharding import PartitionSpec as P


def silu_parts(gate_val):
    sigmoid_val = jax.nn.sigmoid(gate_val)
    return (gate_val * sigmoid_val, sigmoid_val * (1.0 + gate_val * (1.0 - sigmoid_val)))


def slot_layout(routes, experts):
    tok_rows, top_count = routes.shape
    pair_count = tok_rows * top_count
    flat_routes = routes.reshape(pair_count)
    onehot = (flat_routes[:, None] == jnp.arange(experts, dtype=jnp.int32)[None, :]).astype(
        jnp.int32
    )
    before = jnp.cumsum(onehot, axis=0) - onehot
    slot_index = jnp.sum(before * onehot, axis=1)
    capacity = pair_count // experts
    dest_index = flat_routes * capacity + slot_index
    source = (
        jnp.zeros((pair_count,), jnp.int32)
        .at[dest_index]
        .set(jnp.arange(pair_count, dtype=jnp.int32))
    )
    return (dest_index, source, onehot)


def to_experts(rows_in, dp_size, local_experts):
    capacity = rows_in.shape[1]
    width = rows_in.shape[2]
    grouped = rows_in.reshape(dp_size, local_experts, capacity, width)
    return jnp.swapaxes(grouped, 0, 1).reshape(local_experts, dp_size * capacity, width)


def from_experts(values, dp_size):
    local_experts, slot_total, width = values.shape
    capacity = slot_total // dp_size
    grouped = values.reshape(local_experts, dp_size, capacity, width)
    return jnp.swapaxes(grouped, 0, 1).reshape(dp_size * local_experts, capacity, width)


def combine(back_rows, dest_index, factor, tok_rows, top_count):
    width = back_rows.shape[2]
    picked = back_rows.reshape(-1, width)[dest_index].astype(jnp.float32) * factor[:, None]
    return jnp.sum(picked.reshape(tok_rows, top_count, width), axis=1)


def routed_plan(tokens, routes, kept_mask, gate_probs, output_grad, w_gate, w_up, w_down):
    dp_size = lax.axis_size("dp")
    part_count = lax.axis_size("expert")
    local_experts, model_width, hidden_part = w_gate.shape
    experts = local_experts * dp_size
    tok_rows, top_count = routes.shape
    capacity = tok_rows * top_count // experts
    col_width = model_width // part_count
    dest_index, source, onehot = slot_layout(routes, experts)
    keep_float = kept_mask.reshape(-1).astype(jnp.float32)
    weight_flat = keep_float * gate_probs.reshape(-1)
    src_token = source // top_count
    src_keep = keep_float[source]
    src_weight = weight_flat[source]
    col_start = lax.axis_index("expert") * col_width
    token_src = lax.dynamic_slice_in_dim(tokens, col_start, col_width, 1)
    cot_src = lax.dynamic_slice_in_dim(output_grad, col_start, col_width, 1)
    send_width = token_src.shape[1]
    rows_send = (token_src[src_token].astype(jnp.float32) * src_keep[:, None]).astype(jnp.bfloat16)
    rows_send = rows_send.reshape(experts, capacity, send_width)
    cot_send = (cot_src[src_token].astype(jnp.float32) * src_weight[:, None]).astype(jnp.bfloat16)
    cot_send = cot_send.reshape(experts, capacity, send_width)
    totals = jnp.sum(onehot.astype(jnp.float32) * keep_float[:, None], axis=0)
    totals = lax.psum(totals, "dp")
    kept_count = lax.dynamic_slice_in_dim(
        totals, lax.axis_index("dp") * local_experts, local_experts
    )
    rows_in = lax.all_to_all(rows_send, "dp", split_axis=0, concat_axis=0, tiled=True)
    cot_in = lax.all_to_all(cot_send, "dp", split_axis=0, concat_axis=0, tiled=True)
    rows_in = lax.all_gather(rows_in, "expert", axis=2, tiled=True)
    cot_in = lax.all_gather(cot_in, "expert", axis=2, tiled=True)
    expert_in = to_experts(rows_in, dp_size, local_experts)
    cot_full = to_experts(cot_in, dp_size, local_experts)
    down_cols = lax.all_to_all(w_down, "expert", split_axis=2, concat_axis=1, tiled=True)
    gate_rows, up_rows = (
        lax.all_to_all(w_gate, "expert", split_axis=1, concat_axis=2, tiled=True),
        lax.all_to_all(w_up, "expert", split_axis=1, concat_axis=2, tiled=True),
    )
    gate_val = jnp.einsum("lsd,ldh->lsh", expert_in, w_gate, preferred_element_type=jnp.float32)
    up_val = jnp.einsum("lsd,ldh->lsh", expert_in, w_up, preferred_element_type=jnp.float32)
    act_val, act_slope = silu_parts(gate_val)
    hidden = (act_val * up_val).astype(jnp.bfloat16)
    expert_out = jnp.einsum(
        "lsh,lhc->lsc",
        lax.all_gather(hidden, "expert", axis=2, tiled=True),
        down_cols,
        preferred_element_type=jnp.float32,
    ).astype(jnp.bfloat16)
    out_back = lax.all_to_all(
        from_experts(expert_out, dp_size), "dp", split_axis=0, concat_axis=0, tiled=True
    )
    output = combine(out_back, dest_index, weight_flat, tok_rows, top_count).astype(jnp.bfloat16)
    d_hidden = jnp.einsum("lsd,lhd->lsh", cot_full, w_down, preferred_element_type=jnp.float32)
    d_gate = (d_hidden * up_val * act_slope).astype(jnp.bfloat16)
    d_up = (d_hidden * act_val).astype(jnp.bfloat16)
    inv_count = (1.0 / jnp.maximum(kept_count, 1.0))[:, None, None]
    grad_down = (
        jnp.einsum("lsh,lsd->lhd", hidden, cot_full, preferred_element_type=jnp.float32) * inv_count
    ).astype(jnp.bfloat16)
    grad_gate = (
        jnp.einsum("lsd,lsh->ldh", expert_in, d_gate, preferred_element_type=jnp.float32)
        * inv_count
    ).astype(jnp.bfloat16)
    grad_up = (
        jnp.einsum("lsd,lsh->ldh", expert_in, d_up, preferred_element_type=jnp.float32) * inv_count
    ).astype(jnp.bfloat16)
    running = jnp.einsum(
        "lsh,lch->lsc",
        lax.all_gather(d_gate, "expert", axis=2, tiled=True),
        gate_rows,
        preferred_element_type=jnp.float32,
    )
    d_rows = (
        running
        + jnp.einsum(
            "lsh,lch->lsc",
            lax.all_gather(d_up, "expert", axis=2, tiled=True),
            up_rows,
            preferred_element_type=jnp.float32,
        )
    ).astype(jnp.bfloat16)
    grad_back = lax.all_to_all(
        from_experts(d_rows, dp_size), "dp", split_axis=0, concat_axis=0, tiled=True
    )
    input_grad = combine(grad_back, dest_index, keep_float, tok_rows, top_count).astype(
        jnp.bfloat16
    )
    return (output, input_grad, grad_gate, grad_up, grad_down)


def swap(values, axis_name, bit):
    size = lax.axis_size(axis_name)
    return lax.ppermute(values, axis_name, [(i, i ^ bit) for i in range(size)])


def shift(values, steps):
    size = lax.axis_size("dp")
    return lax.ppermute(values, "dp", [(i, (i + 4 * steps) % size) for i in range(size)])


def cut_halves(part_ref, tokens, cots, table, mine, other, table_out):
    table_out[...] = table[...]
    rows = tokens.shape[0] // 2
    own = pl.multiple_of(part_ref[0] * rows, rows)
    rest = pl.multiple_of(rows - part_ref[0] * rows, rows)
    for kind, values in enumerate((tokens, cots)):
        mine[kind] = values[pl.ds(own, rows), :]
        other[kind] = values[pl.ds(rest, rows), :]


def own_halves(part_arg, tokens, cots, table):
    shape = jax.ShapeDtypeStruct((2, tokens.shape[0] // 2, tokens.shape[1]), tokens.dtype)
    vmem = pl.BlockSpec(memory_space=pltpu.VMEM)
    return call_kernel(
        cut_halves,
        "own_halves",
        [shape, shape, jax.ShapeDtypeStruct(table.shape, table.dtype)],
        [part_arg, tokens, cots, table],
        in_specs=[pl.BlockSpec(memory_space=pltpu.SMEM), vmem, vmem, vmem],
    )


def cut_kinds(rest, across, *refs):
    rest_out, across_out, mark, sems = refs[-4:]
    mark[...] = jnp.zeros_like(mark)
    copies = [
        pltpu.make_async_copy(rest.at[0], rest_out, sems.at[0]),
        pltpu.make_async_copy(across.at[1], across_out, sems.at[1]),
    ]
    for copy in copies:
        copy.start()
    for copy in copies:
        copy.wait()


def kinds_apart(rest, across, after):
    hbm = pl.BlockSpec(memory_space=pl.ANY)
    shape = jax.ShapeDtypeStruct(rest.shape[1:], rest.dtype)
    return call_kernel(
        cut_kinds,
        "cut_kinds",
        [shape, shape, jax.ShapeDtypeStruct((8, 128), jnp.float32)],
        [rest, across, *after],
        in_specs=[hbm] * (2 + len(after)),
        scratch_shapes=[pltpu.SemaphoreType.DMA((2,))],
    )


def gather_line(mine, other, line, run_first):
    halves = [mine]
    for _ in range(line - 1):
        halves.append(shift(halves[-1], 1))
    steps = []
    for step, half in enumerate(halves):
        rest = swap(half, "expert", 1) if step else other
        across = swap(half, "dp", 2)
        if step:
            after = [run_first(steps[0])] if step == line - 1 else []
            tokens, cots, _ = kinds_apart(rest, across, after)
            last = (swap(tokens, "dp", 2), swap(cots, "expert", 1))
        else:
            last = (swap(across, "expert", 1),)
        pieces = (half, rest, across) + last
        steps.append(pieces + tuple(swap(piece, "dp", 1) for piece in pieces))
    return steps


def gather_small(values, line):
    lines = jnp.stack([values] + [shift(values, step) for step in range(1, line)])
    pairs = jnp.stack([lines, swap(lines, "dp", 2)], axis=1)
    return jnp.stack([pairs, swap(pairs, "dp", 1)], axis=2)


def mxu(a, b, dims=((1,), (0,))):
    return lax.dot_general(a, b, (dims, ((), ())), preferred_element_type=jnp.float32)


def add_to(target, *terms):
    target[...] = sum(term.astype(jnp.float32) for term in terms).astype(jnp.bfloat16)


def add_cores(keep, got, *refs):
    away_out, away_grad, home, mark = refs[-4:]
    mark[...] = jnp.zeros_like(mark)
    add_to(away_out, keep[0, 1], got[0, 1])
    add_to(away_grad, keep[1, 1], got[1, 1])
    add_to(home, keep[:, 0], got[:, 0])


def add_first(home, away_out, away_grad, *refs):
    last_out, last_grad, mark = refs[-3:]
    mark[...] = jnp.zeros_like(mark)
    add_to(last_out, home[0, 1], away_out[1])
    add_to(last_grad, home[1, 1], away_grad[1])


def add_last(extra_count, home, away_out, away_grad, last_out, last_grad, *refs):
    total, mark = refs[-2:]
    extra = refs[:extra_count]
    mark[...] = jnp.zeros_like(mark)
    add_to(total.at[0], home[0, 0], away_out[0], last_out[...], *[e[0] for e in extra])
    add_to(total.at[1], home[1, 0], away_grad[0], last_grad[...], *[e[1] for e in extra])


def call_kernel(kernel, name, shapes, args, flops=0, vmem=8 * 2**20, **options):
    space = pl.BlockSpec(memory_space=pltpu.VMEM)
    moved = sum(math.prod(a.shape) * a.dtype.itemsize for a in [*args, *shapes])
    return pl.pallas_call(
        kernel,
        out_shape=shapes,
        in_specs=options.pop("in_specs", [space] * len(args)),
        out_specs=options.pop("out_specs", [space] * len(shapes)),
        compiler_params=pltpu.CompilerParams(vmem_limit_bytes=vmem),
        cost_estimate=pl.CostEstimate(flops=flops, bytes_accessed=moved, transcendentals=0),
        name=name,
        **options,
    )(*args)


def send_home(keep, send, extra, before):
    def array(*shape):
        return jax.ShapeDtypeStruct(shape, jnp.bfloat16)

    rows, columns = keep.shape[3:]
    pair, single = array(2, rows, columns), array(rows, columns)
    mark = jax.ShapeDtypeStruct((8, 128), jnp.float32)
    got = swap(send, "dp", 1)
    away_out, away_grad, home, mark_cores = call_kernel(
        add_cores, "add_cores", [pair, pair, array(2, 2, rows, columns), mark], [keep, got]
    )
    away = (swap(away_out, "dp", 2), swap(away_grad, "expert", 1))
    *lasts, mark_first = call_kernel(add_first, "add_first", [single, single, mark], [home, *away, *before])
    last = (swap(lasts[0], "expert", 1), swap(lasts[1], "dp", 2))
    total, mark_last = call_kernel(
        functools.partial(add_last, len(extra)),
        "add_last",
        [pair, mark],
        [home, *away, *last, *extra],
    )
    return total, mark_last


def take_rows(kind, pick_ref, pieces, store):
    for x in range(2):
        for core in range(2):
            half, rest, across, *last = pieces[core * len(pieces) // 2 : (core + 1) * len(pieces) // 2]
            if x == 0:
                block = jnp.concatenate([half[kind], rest[kind]], axis=0)
            else:
                rows = last[kind][...] if len(last) == 2 else last[0][kind]
                block = jnp.concatenate([across[kind], rows], axis=0)
            store(2 * x + core, mxu(pick_ref[x, core], block))


def spread_rows(kind, part, half, rows, place_ref, keep_ref, send_ref):
    capacity = rows.shape[0] // 4
    side = half ^ part
    for x in range(2):
        for core in range(2):
            group = 2 * x + core
            piece = rows[group * capacity : (group + 1) * capacity]
            out = mxu(place_ref[x, core], piece).astype(jnp.bfloat16)
            target = keep_ref if core == 0 else send_ref
            if kind == 0:
                target[kind, x, side] = out
            else:
                target[kind, side, x] = out


def chunk_kernel(step, count, part_ref, pick_ref, place_ref, scale_ref, *refs):
    sources, refs = refs[:count], refs[-17 - count :]
    outs, saved = refs[:2], refs[2:7]
    kept, buffers = refs[7:12], refs[12 : 12 + count]
    homes, sems = refs[-5:-3], refs[-3:]
    keep_ref, send_ref = homes
    rows_ref, cot_ref, hidden_ref, d_gate_ref, d_up_ref = kept
    pieces, (w_gate, w_up, w_down) = buffers[:-3], buffers[-3:]
    rows, capacity = rows_ref.shape[0], pick_ref.shape[2]
    def piece_loads(kind):
        copies = []
        for i, (source, target) in enumerate(zip(sources[:-3], pieces)):
            if len(source.shape) == 3:
                source, target = source.at[kind], target.at[kind]
            elif i % 5 != 3 + kind:
                continue
            copies.append(pltpu.make_async_copy(source, target, sems[0].at[kind, i]))
        return copies

    weight_loads = [
        pltpu.make_async_copy(source, target, sems[0].at[0, count - 3 + i])
        for i, (source, target) in enumerate(zip(sources[-3:], buffers[-3:]))
    ]
    stores = [
        pltpu.make_async_copy(source, target.at[pl.ds(step * rows, rows)], sems[1].at[i])
        for i, (source, target) in enumerate(zip(kept, saved))
    ]
    sends = [
        pltpu.make_async_copy(source.at[kind], target.at[kind], sems[2].at[kind, i])
        for kind in range(2)
        for i, (source, target) in enumerate(zip(homes, outs))
    ]
    token_loads, cot_loads = piece_loads(0), piece_loads(1)
    for copy in [*token_loads, *weight_loads[:2], weight_loads[2], *cot_loads]:
        copy.start()

    def store_rows(group, found):
        rows_ref[pl.ds(group * capacity, capacity), :] = found.astype(jnp.bfloat16)

    def store_cot(group, found):
        span = pl.ds(group * capacity, capacity)
        cot_ref[span, :] = (found * scale_ref[span, :]).astype(jnp.bfloat16)

    part = part_ref[0]
    width = w_down.shape[1] // 2
    halves = [slice(half * width, (half + 1) * width) for half in range(2)]
    for copy in token_loads:
        copy.wait()
    take_rows(0, pick_ref, pieces, store_rows)
    stores[0].start()
    expert_in = rows_ref[...]
    weight_loads[0].wait()
    gate_val = mxu(expert_in, w_gate[...])
    weight_loads[1].wait()
    up_val = mxu(expert_in, w_up[...])
    act_val, act_slope = silu_parts(gate_val)
    hidden = (act_val * up_val).astype(jnp.bfloat16)
    hidden_ref[...] = hidden
    stores[2].start()
    weight_loads[2].wait()
    for half, span in enumerate(halves):
        out = (mxu(hidden, w_down[:, span]) * scale_ref[...]).astype(jnp.bfloat16)
        spread_rows(0, part, half, out, place_ref, keep_ref, send_ref)
    for send in sends[:2]:
        send.start()
    for copy in cot_loads:
        copy.wait()
    take_rows(1, pick_ref, pieces, store_cot)
    stores[1].start()
    d_hidden = mxu(cot_ref[...], w_down[...], ((1,), (1,)))
    d_gate = (d_hidden * up_val * act_slope).astype(jnp.bfloat16)
    d_up = (d_hidden * act_val).astype(jnp.bfloat16)
    d_gate_ref[...] = d_gate
    d_up_ref[...] = d_up
    stores[3].start()
    stores[4].start()
    for half, span in enumerate(halves):
        grad = mxu(d_gate, w_gate[span, :], ((1,), (1,))) + mxu(d_up, w_up[span, :], ((1,), (1,)))
        spread_rows(1, part, half, grad.astype(jnp.bfloat16), place_ref, keep_ref, send_ref)
    for send in sends[2:]:
        send.start()
    for copy in stores + sends:
        copy.wait()


def run_chunk(step, tables, sources, saved_shapes, saved, marks):
    def array(a):
        return jax.ShapeDtypeStruct(a.shape, a.dtype)

    def scratch(a):
        return pltpu.VMEM(a.shape, a.dtype)

    kinds, half_rows, model_width = sources[0].shape
    home = jax.ShapeDtypeStruct((kinds, 2, 2, 2 * half_rows, model_width // 2), jnp.bfloat16)
    vmem, hbm = pl.BlockSpec(memory_space=pltpu.VMEM), pl.BlockSpec(memory_space=pl.ANY)
    rows = tables[-1].shape[0]
    first_saved = len(tables) + len(sources)
    return call_kernel(
        functools.partial(chunk_kernel, step, len(sources)),
        "chunk",
        [home, home, *saved_shapes],
        [*tables, *sources, *saved, *marks],
        vmem=60 * 2**20,
        flops=12 * rows * sources[-1].shape[0] * sources[-1].shape[1],
        in_specs=[pl.BlockSpec(memory_space=pltpu.SMEM)]
        + [vmem] * (len(tables) - 1)
        + [hbm] * (len(sources) + len(saved))
        + [vmem] * len(marks),
        out_specs=[hbm] * (2 + len(saved_shapes)),
        input_output_aliases={first_saved + i: 2 + i for i in range(len(saved))},
        scratch_shapes=[pltpu.VMEM((rows, s.shape[1]), s.dtype) for s in saved_shapes]
        + [scratch(source) for source in sources]
        + [scratch(home)] * 2
        + [pltpu.SemaphoreType.DMA(n) for n in ((2, len(sources)), (len(saved_shapes),), (2, 2))],
    )


def dense_plan(tokens, routes, kept_mask, gate_probs, output_grad, w_gate, w_up, w_down):
    dp_size = lax.axis_size("dp")
    line = dp_size // 4
    tok_rows, top_count = routes.shape
    capacity = tok_rows * top_count // dp_size
    model_width = tokens.shape[1]
    hidden_part = w_gate.shape[2]
    rows = 4 * capacity
    part = lax.axis_index("expert")
    w_gate, w_up, w_down = w_gate[0], w_up[0], w_down[0]

    table = jnp.concatenate(
        [routes.T.astype(jnp.float32), kept_mask.T.astype(jnp.float32), gate_probs.T], axis=0
    )
    part_arg = part.astype(jnp.int32).reshape(1)
    mine, other, table = own_halves(part_arg, tokens, output_grad, table)
    table = gather_small(table, line)
    chosen, kept, probs = jnp.split(table, 3, axis=3)
    expert = lax.axis_index("dp").astype(jnp.float32)
    hit = jnp.where(chosen == expert, kept, 0.0)
    used = jnp.sum(hit, axis=3)
    weight = jnp.sum(hit * probs, axis=3)
    kept_count = jnp.sum(used)
    earlier = jnp.triu(jnp.ones((tok_rows, tok_rows), jnp.bfloat16), 1)
    rank = jnp.einsum(
        "sabt,tu->sabu", used.astype(jnp.bfloat16), earlier, preferred_element_type=jnp.float32
    )
    slots = jnp.arange(capacity, dtype=jnp.float32)[:, None]
    pick = jnp.where(rank[..., None, :] == slots, used[..., None, :], 0.0)
    row_weight = jnp.sum(pick * weight[..., None, :], axis=4).reshape(line, rows, 1)
    pick = pick.astype(jnp.bfloat16)
    place = jnp.swapaxes(pick, 3, 4)
    pick_in = jnp.where(part == 0, pick, jnp.roll(pick, tok_rows // 2, axis=4))


    def saved_array(width):
        return jax.ShapeDtypeStruct((line * rows, width), jnp.bfloat16)

    saved_shapes = [saved_array(model_width)] * 2 + [saved_array(hidden_part)] * 3
    done = []

    def chunk(step, rows_in):
        saved = done[-1][2:] if done else []
        done.append(
            run_chunk(
                step,
                [part_arg, pick_in[step], place[step], row_weight[step]],
                [*rows_in, w_gate, w_up, w_down],
                saved_shapes,
                saved,
                [],
            )
        )
        return done[-1][1]

    pieces = gather_line(mine, other, line, functools.partial(chunk, 0))
    for step in range(1, line):
        chunk(step, pieces[step])
    saved = done[-1][2:]

    down, up, before = [], [], []
    for step in range(line // 2, 0, -1):
        total, mark = send_home(*done[step][:2], down, [])
        before = before or [mark]
        down = [shift(total, -1)]
    for step in range(line // 2 + 1, line):
        up = [shift(send_home(*done[step][:2], up, before)[0], 1)]
    returns = [send_home(*done[0][:2], [], [])[0], *down, *up]
    expert_in, cot_rows, hidden, d_gate, d_up = saved
    inv_count = 1.0 / jnp.maximum(kept_count, 1.0)
    by_row = ((0,), (0,))
    grad_down = (mxu(hidden, cot_rows, by_row) * inv_count).astype(jnp.bfloat16)
    grad_gate = (mxu(expert_in, d_gate, by_row) * inv_count).astype(jnp.bfloat16)
    grad_up = (mxu(expert_in, d_up, by_row) * inv_count).astype(jnp.bfloat16)
    results = sum(total.astype(jnp.float32) for total in returns).astype(jnp.bfloat16)
    return (results[0], results[1], grad_gate[None], grad_up[None], grad_down[None])


def per_device(tokens, routes, kept_mask, gate_probs, output_grad, w_gate, w_up, w_down):
    dp_size = lax.axis_size("dp")
    local_experts = w_gate.shape[0]
    top_count = routes.shape[1]
    dense = (
        local_experts == 1
        and lax.axis_size("expert") == 2
        and dp_size % 4 == 0
        and 2 * top_count >= dp_size
    )
    plan = dense_plan if dense else routed_plan
    return plan(tokens, routes, kept_mask, gate_probs, output_grad, w_gate, w_up, w_down)


def solution(mesh):
    placed = (
        P("dp", None),
        P("dp", None),
        P("dp", None),
        P("dp", None),
        P("dp", None),
        P("dp", None, "expert"),
        P("dp", None, "expert"),
        P("dp", "expert", None),
    )
    return jax.shard_map(
        per_device,
        mesh=mesh,
        in_specs=placed,
        out_specs=(
            P("dp", "expert"),
            P("dp", "expert"),
            P("dp", None, "expert"),
            P("dp", None, "expert"),
            P("dp", "expert", None),
        ),
        check_vma=False,
    )
```

profile of v0, /device:TPU:0, one launch (start us, length us, event | category | flops | bytes accessed | tf_op | source)
XLA Modules:
  0.0 239.5 jit_solution(14019563528449465998)
XLA Ops:
  4.2 3.1 %collective-permute-start.16 = (bf16[2,64,2048]{2,1,0:T(8,128)(2,1)S(1)}, bf16[2,64,2048]{2,1,0:T(8,128)(2,1)S(1)}, u32[]{:S(2)}, u32[]{:S(2)}) collective-permute-start(bf16[2,64,2048]{2,1,0:T(8,128)(2,1)S(1)} %get-tuple-element.68.refs_0_), channel_id=1, source_target_pairs={{0,8},{2,10},{4,12},{6,14},{8,16},{10,18},{12,20},{14,22},{16,24},... | collective-permute-start | bytes 1572872 | tf_op jit(solution)/shard_map/ppermute | solution.py:153
  8.8 12.5 %collective-permute-done.16.refs_0_ = bf16[2,64,2048]{2,1,0:T(8,128)(2,1)S(1)} collective-permute-done((bf16[2,64,2048]{2,1,0:T(8,128)(2,1)S(1)}, bf16[2,64,2048]{2,1,0:T(8,128)(2,1)S(1)}, u32[]{:S(2)}, u32[]{:S(2)}) %collective-permute-start.16) | collective-permute-done | bytes 524320 | tf_op jit(solution)/shard_map/ppermute | solution.py:153
  24.5 2.0 collective-permute-done.2
  26.4 2.6 %collective-permute-done.1 = f32[24,128]{1,0:T(8,128)S(1)} collective-permute-done((f32[24,128]{1,0:T(8,128)S(1)}, f32[24,128]{1,0:T(8,128)S(1)}, u32[]{:S(2)}, u32[]{:S(2)}) %collective-permute-start.1) | collective-permute-done | bytes 12320 | tf_op jit(solution)/shard_map/ppermute | solution.py:153
  29.1 2.9 %collective-permute-done = f32[24,128]{1,0:T(8,128)S(1)} collective-permute-done((f32[24,128]{1,0:T(8,128)S(1)}, f32[24,128]{1,0:T(8,128)S(1)}, u32[]{:S(2)}, u32[]{:S(2)}) %collective-permute-start) | collective-permute-done | bytes 12320 | tf_op jit(solution)/shard_map/ppermute | solution.py:153
  34.1 2.0 collective-permute-done.3
  40.6 2.3 collective-permute-done.17.rest.refs_1_
  46.4 7.3 %collective-permute-done.31.refs_0_ = bf16[2,64,2048]{2,1,0:T(8,128)(2,1)S(1)} collective-permute-done((bf16[2,64,2048]{2,1,0:T(8,128)(2,1)S(1)}, bf16[2,64,2048]{2,1,0:T(8,128)(2,1)S(1)}, u32[]{:S(2)}, u32[]{:S(2)}) %collective-permute-start.31) | collective-permute-done | bytes 524320 | tf_op jit(solution)/shard_map/ppermute | solution.py:153
  58.0 5.0 %collective-permute-done.20.refs_4_ = bf16[64,2048]{1,0:T(8,128)(2,1)} collective-permute-done((bf16[64,2048]{1,0:T(8,128)(2,1)S(1)}, bf16[64,2048]{1,0:T(8,128)(2,1)}, u32[]{:S(2)}, u32[]{:S(2)}) %collective-permute-start.20) | collective-permute-done | bytes 262176 | tf_op jit(solution)/shard_map/ppermute | solution.py:148
  63.8 4.5 %collective-permute-done.33.across.refs_2_ = bf16[2,64,2048]{2,1,0:T(8,128)(2,1)S(1)} collective-permute-done((bf16[2,64,2048]{2,1,0:T(8,128)(2,1)S(1)}, bf16[2,64,2048]{2,1,0:T(8,128)(2,1)S(1)}, u32[]{:S(2)}, u32[]{:S(2)}) %collective-permute-start.33) | collective-permute-done | bytes 524320 | tf_op jit(solution)/shard_map/ppermute | solution.py:148
  69.2 3.4 %collective-permute-done.32.rest.refs_1_ = bf16[2,64,2048]{2,1,0:T(8,128)(2,1)S(1)} collective-permute-done((bf16[2,64,2048]{2,1,0:T(8,128)(2,1)S(1)}, bf16[2,64,2048]{2,1,0:T(8,128)(2,1)S(1)}, u32[]{:S(2)}, u32[]{:S(2)}) %collective-permute-start.32) | collective-permute-done | bytes 524320 | tf_op jit(solution)/shard_map/ppermute | solution.py:148
  84.4 10.7 %chunk.4 = (bf16[2,2,2,128,1024]{4,3,2,1,0:T(8,128)(2,1)}, bf16[2,2,2,128,1024]{4,3,2,1,0:T(8,128)(2,1)}, bf16[1024,2048]{1,0:T(8,128)(2,1)}, bf16[1024,2048]{1,...) custom-call(s32[1]{0:T(128)} %bitcast.part_ref, ...), custom_call_target="tpu_custom_call" | custom-call | flops 3221225472 | bytes 26346500 | tf_op jit(solution)/shard_map/chunk/pallas_call | solution.py:263
  95.8 10.7 %chunk.5 = (bf16[2,2,2,128,1024]{4,3,2,1,0:T(8,128)(2,1)}, bf16[2,2,2,128,1024]{4,3,2,1,0:T(8,128)(2,1)}, bf16[1024,2048]{1,0:T(8,128)(2,1)}, bf16[1024,2048]{1,...) custom-call(s32[1]{0:T(128)} %bitcast.part_ref, ...), custom_call_target="tpu_custom_call", output_to_operand_aliasing={{2}: (17, {}), {3}: (18, {}), {4}: (19, {}), {5}: (20, {}),... | custom-call | flops 3221225472 | bytes 37880836 | tf_op jit(solution)/shard_map/chunk/pallas_call | solution.py:263
  110.0 10.8 %chunk.6 = (bf16[2,2,2,128,1024]{4,3,2,1,0:T(8,128)(2,1)}, bf16[2,2,2,128,1024]{4,3,2,1,0:T(8,128)(2,1)}, bf16[1024,2048]{1,0:T(8,128)(2,1)}, bf16[1024,2048]{1,...) custom-call(s32[1]{0:T(128)} %bitcast.part_ref, ...), custom_call_target="tpu_custom_call", output_to_operand_aliasing={{2}: (17, {}), {3}: (18, {}), {4}: (19, {}), {5}: (20, {}),... | custom-call | flops 3221225472 | bytes 37880836 | tf_op jit(solution)/shard_map/chunk/pallas_call | solution.py:263
  123.2 6.6 %collective-permute-done.52.refs_4_ = bf16[64,2048]{1,0:T(8,128)(2,1)} collective-permute-done((bf16[64,2048]{1,0:T(8,128)(2,1)S(1)}, bf16[64,2048]{1,0:T(8,128)(2,1)}, u32[]{:S(2)}, u32[]{:S(2)}) %collective-permute-start.52) | collective-permute-done | bytes 262176 | tf_op jit(solution)/shard_map/ppermute | solution.py:148
  131.8 10.8 %chunk.7 = (bf16[2,2,2,128,1024]{4,3,2,1,0:T(8,128)(2,1)}, bf16[2,2,2,128,1024]{4,3,2,1,0:T(8,128)(2,1)}, bf16[1024,2048]{1,0:T(8,128)(2,1)}, bf16[1024,2048]{1,...) custom-call(s32[1]{0:T(128)} %bitcast.part_ref, ...), custom_call_target="tpu_custom_call", output_to_operand_aliasing={{2}: (17, {}), {3}: (18, {}), {4}: (19, {}), {5}: (20, {}),... | custom-call | flops 3221225472 | bytes 37880836 | tf_op jit(solution)/shard_map/chunk/pallas_call | solution.py:263
  150.1 2.7 %add_cores.5 = (bf16[2,128,1024]{2,1,0:T(8,128)(2,1)}, bf16[2,128,1024]{2,1,0:T(8,128)(2,1)}, bf16[2,2,128,1024]{3,2,1,0:T(8,128)(2,1)S(1)}, f32[8,128]{1,0:T(8,128)}) custom-call(bf16[2,2,2,128,1024]{4,3,2,1,0:T(8,128)(2,1)S(1)} %copy-done.5, bf16[2,2,2,128,1024]{4,3,2,1,0:T(8,128)(2,1)} %collective-permute-done.26.got), custom_call_target="tpu_custom_call" | custom-call | bytes 6295552 | tf_op jit(solution)/shard_map/add_cores/pallas_call | solution.py:263
  154.5 8.6 %collective-permute-done.42.away_out = bf16[2,128,1024]{2,1,0:T(8,128)(2,1)S(1)} collective-permute-done((bf16[2,128,1024]{2,1,0:T(8,128)(2,1)S(1)}, bf16[2,128,1024]{2,1,0:T(8,128)(2,1)S(1)}, u32[]{:S(2)}, u32[]{:S(2)}) %collective-permute-start.42) | collective-permute-done | bytes 524320 | tf_op jit(solution)/shard_map/ppermute | solution.py:148
  168.8 2.3 add_cores.4
  173.0 2.2 add_cores.7
  178.6 5.1 %collective-permute-done.44.last_out = bf16[128,1024]{1,0:T(8,128)(2,1)S(1)} collective-permute-done((bf16[128,1024]{1,0:T(8,128)(2,1)}, bf16[128,1024]{1,0:T(8,128)(2,1)S(1)}, u32[]{:S(2)}, u32[]{:S(2)}) %collective-permute-start.44) | collective-permute-done | bytes 262176 | tf_op jit(solution)/shard_map/ppermute | solution.py:148
  185.2 3.8 %fusion = bf16[1,2048,512]{2,1,0:T(8,128)(2,1)} fusion(bf16[1024,2048]{1,0:T(8,128)(2,1)S(1)} %copy-done.18, bf16[1024,512]{1,0:T(8,128)(2,1)S(1)} %copy-done.21, f32[]{:T(128)S(6)} %div.3), kind=kOutput, calls=%fused_computation.3 | convolution fusion | flops 2149580800 | bytes 7340036 | tf_op jit(solution)/shard_map/dot_general | solution.py:230
  189.0 1.9 add_first.5
  193.3 8.1 %collective-permute-done.59.away_out = bf16[2,128,1024]{2,1,0:T(8,128)(2,1)S(1)} collective-permute-done((bf16[2,128,1024]{2,1,0:T(8,128)(2,1)S(1)}, bf16[2,128,1024]{2,1,0:T(8,128)(2,1)S(1)}, u32[]{:S(2)}, u32[]{:S(2)}) %collective-permute-start.59) | collective-permute-done | bytes 524320 | tf_op jit(solution)/shard_map/ppermute | solution.py:148
  201.8 4.4 %collective-permute-done.60.away_grad = bf16[2,128,1024]{2,1,0:T(8,128)(2,1)S(1)} collective-permute-done((bf16[2,128,1024]{2,1,0:T(8,128)(2,1)S(1)}, bf16[2,128,1024]{2,1,0:T(8,128)(2,1)S(1)}, u32[]{:S(2)}, u32[]{:S(2)}) %collective-permute-start.60) | collective-permute-done | bytes 524320 | tf_op jit(solution)/shard_map/ppermute | solution.py:148
  206.2 2.1 collective-permute-start.46
  210.8 3.8 %fusion.1 = bf16[1,2048,512]{2,1,0:T(8,128)(2,1)} fusion(bf16[1024,2048]{1,0:T(8,128)(2,1)S(1)} %copy-done.18, bf16[1024,512]{1,0:T(8,128)(2,1)S(1)} %copy-done.22, f32[]{:T(128)S(6)} %div.3), kind=kOutput, calls=%fused_computation.4 | convolution fusion | flops 2149580800 | bytes 7340036 | tf_op jit(solution)/shard_map/dot_general | solution.py:230
  217.4 1.8 add_last.6
  219.2 2.4 collective-permute-start.47
  222.2 3.8 %fusion.2 = bf16[1,512,2048]{2,1,0:T(8,128)(2,1)} fusion(bf16[1024,512]{1,0:T(8,128)(2,1)S(1)} %copy-done.20, bf16[1024,2048]{1,0:T(8,128)(2,1)S(1)} %copy-done.19, f32[]{:T(128)S(6)} %div.3), kind=kOutput, calls=%fused_computation.5 | convolution fusion | flops 2149580800 | bytes 7340036 | tf_op jit(solution)/shard_map/dot_general | solution.py:230
  226.6 5.7 %collective-permute-done.47 = bf16[2,128,1024]{2,1,0:T(8,128)(2,1)S(1)} collective-permute-done((bf16[2,128,1024]{2,1,0:T(8,128)(2,1)S(1)}, bf16[2,128,1024]{2,1,0:T(8,128)(2,1)S(1)}, u32[]{:S(2)}, u32[]{:S(2)}) %collective-permute-start.47) | collective-permute-done | bytes 524320 | tf_op jit(solution)/shard_map/ppermute | solution.py:153
  232.3 5.6 %collective-permute-done.63 = bf16[2,128,1024]{2,1,0:T(8,128)(2,1)S(1)} collective-permute-done((bf16[2,128,1024]{2,1,0:T(8,128)(2,1)S(1)}, bf16[2,128,1024]{2,1,0:T(8,128)(2,1)S(1)}, u32[]{:S(2)}, u32[]{:S(2)}) %collective-permute-start.63) | collective-permute-done | bytes 524320 | tf_op jit(solution)/shard_map/ppermute | solution.py:153
  (212 shorter events, 76.1 us)
Async XLA Ops:
  4.2 17.0 %collective-permute-start.16 = (bf16[2,64,2048]{2,1,0:T(8,128)(2,1)S(1)}, bf16[2,64,2048]{2,1,0:T(8,128)(2,1)S(1)}, u32[]{:S(2)}, u32[]{:S(2)}) collective-permute-start(bf16[2,64,2048]{2,1,0:T(8,128)(2,1)S(1)} %get-tuple-element.68.refs_0_), channel_id=1, source_target_pairs={{0,8},{2,10},{4,12},{6,14},{8,16},{10,18},{12,20},{14,22},{16,24},... | collective-permute-start | bytes 1572872 | tf_op jit(solution)/shard_map/ppermute | solution.py:153
  7.3 30.4 %collective-permute-start.8 = (bf16[2,64,2048]{2,1,0:T(8,128)(2,1)S(1)}, bf16[2,64,2048]{2,1,0:T(8,128)(2,1)S(1)}, u32[]{:S(2)}, u32[]{:S(2)}) collective-permute-start(bf16[2,64,2048]{2,1,0:T(8,128)(2,1)S(1)} %get-tuple-element.69.refs_1_), channel_id=1, source_target_pairs={{0,2},{2,0},{4,6},{6,4},{8,10},{10,8},{12,14},{14,12},{16,18},{18,... | collective-permute-start | bytes 1572872 | tf_op jit(solution)/shard_map/ppermute | solution.py:148
  7.3 30.4 %collective-permute-start.5 = (bf16[2,64,2048]{2,1,0:T(8,128)(2,1)S(1)}, bf16[2,64,2048]{2,1,0:T(8,128)(2,1)S(1)}, u32[]{:S(2)}, u32[]{:S(2)}) collective-permute-start(bf16[2,64,2048]{2,1,0:T(8,128)(2,1)S(1)} %get-tuple-element.68.refs_0_), channel_id=1, source_target_pairs={{0,4},{2,6},{4,0},{6,2},{8,12},{10,14},{12,8},{14,10},{16,20},{18,... | collective-permute-start | bytes 1572872 | tf_op jit(solution)/shard_map/ppermute | solution.py:148
  21.2 19.0 %collective-permute-start.18 = (bf16[2,64,2048]{2,1,0:T(8,128)(2,1)S(1)}, bf16[2,64,2048]{2,1,0:T(8,128)(2,1)S(1)}, u32[]{:S(2)}, u32[]{:S(2)}) collective-permute-start(bf16[2,64,2048]{2,1,0:T(8,128)(2,1)S(1)} %collective-permute-done.16.refs_0_), channel_id=1, source_target_pairs={{0,4},{2,6},{4,0},{6,2},{8,12},{10,14},{12,8},{14,10},{16,20},{18,... | collective-permute-start | bytes 1572872 | tf_op jit(solution)/shard_map/ppermute | solution.py:148
  37.6 16.0 %collective-permute-start.31 = (bf16[2,64,2048]{2,1,0:T(8,128)(2,1)S(1)}, bf16[2,64,2048]{2,1,0:T(8,128)(2,1)S(1)}, u32[]{:S(2)}, u32[]{:S(2)}) collective-permute-start(bf16[2,64,2048]{2,1,0:T(8,128)(2,1)S(1)} %collective-permute-done.16.refs_0_), channel_id=1, source_target_pairs={{0,8},{2,10},{4,12},{6,14},{8,16},{10,18},{12,20},{14,22},{16,24},... | collective-permute-start | bytes 1572872 | tf_op jit(solution)/shard_map/ppermute | solution.py:153
  39.2 15.9 %collective-permute-start.21 = (bf16[2,64,2048]{2,1,0:T(8,128)(2,1)S(1)}, bf16[2,64,2048]{2,1,0:T(8,128)(2,1)S(1)}, u32[]{:S(2)}, u32[]{:S(2)}) collective-permute-start(bf16[2,64,2048]{2,1,0:T(8,128)(2,1)S(1)} %collective-permute-done.16.refs_0_), channel_id=1, source_target_pairs={{0,2},{2,0},{4,6},{6,4},{8,10},{10,8},{12,14},{14,12},{16,18},{18,... | collective-permute-start | bytes 1572872 | tf_op jit(solution)/shard_map/ppermute | solution.py:148
  40.2 15.7 %collective-permute-start.9 = (bf16[2,64,2048]{2,1,0:T(8,128)(2,1)}, bf16[2,64,2048]{2,1,0:T(8,128)(2,1)S(1)}, u32[]{:S(2)}, u32[]{:S(2)}) collective-permute-start(bf16[2,64,2048]{2,1,0:T(8,128)(2,1)} %copy-done.33), channel_id=1, source_target_pairs={{0,2},{2,0},{4,6},{6,4},{8,10},{10,8},{12,14},{14,12},{16,18},{18,... | collective-permute-start | bytes 1572872 | tf_op jit(solution)/shard_map/ppermute | solution.py:148
  42.9 14.9 %collective-permute-start.6 = (bf16[2,64,2048]{2,1,0:T(8,128)(2,1)}, bf16[2,64,2048]{2,1,0:T(8,128)(2,1)}, u32[]{:S(2)}, u32[]{:S(2)}) collective-permute-start(bf16[2,64,2048]{2,1,0:T(8,128)(2,1)} %copy-done.33), channel_id=1, source_target_pairs={{0,1},{1,0},{2,3},{3,2},{4,5},{5,4},{6,7},{7,6},{8,9},{9,8},{10,11... | collective-permute-start | bytes 1572872 | tf_op jit(solution)/shard_map/ppermute | solution.py:148
  56.7 15.9 %collective-permute-start.32 = (bf16[2,64,2048]{2,1,0:T(8,128)(2,1)S(1)}, bf16[2,64,2048]{2,1,0:T(8,128)(2,1)S(1)}, u32[]{:S(2)}, u32[]{:S(2)}) collective-permute-start(bf16[2,64,2048]{2,1,0:T(8,128)(2,1)S(1)} %collective-permute-done.31.refs_0_), channel_id=1, source_target_pairs={{0,1},{1,0},{2,3},{3,2},{4,5},{5,4},{6,7},{7,6},{8,9},{9,8},{10,11... | collective-permute-start | bytes 1572872 | tf_op jit(solution)/shard_map/ppermute | solution.py:148
  57.9 15.9 %collective-permute-start.48 = (bf16[2,64,2048]{2,1,0:T(8,128)(2,1)S(1)}, bf16[2,64,2048]{2,1,0:T(8,128)(2,1)}, u32[]{:S(2)}, u32[]{:S(2)}) collective-permute-start(bf16[2,64,2048]{2,1,0:T(8,128)(2,1)S(1)} %collective-permute-done.31.refs_0_), channel_id=1, source_target_pairs={{0,8},{2,10},{4,12},{6,14},{8,16},{10,18},{12,20},{14,22},{16,24},... | collective-permute-start | bytes 1572872 | tf_op jit(solution)/shard_map/ppermute | solution.py:153
  57.9 16.4 %collective-permute-start.23 = (bf16[2,64,2048]{2,1,0:T(8,128)(2,1)S(1)}, bf16[2,64,2048]{2,1,0:T(8,128)(2,1)S(1)}, u32[]{:S(2)}, u32[]{:S(2)}) collective-permute-start(bf16[2,64,2048]{2,1,0:T(8,128)(2,1)S(1)} %collective-permute-done.18.across.refs_2_), channel_id=1, source_target_pairs={{0,2},{2,0},{4,6},{6,4},{8,10},{10,8},{12,14},{14,12},{16,18},{18,... | collective-permute-start | bytes 1572872 | tf_op jit(solution)/shard_map/ppermute | solution.py:148
  78.9 16.3 %collective-permute-start.50 = (bf16[2,64,2048]{2,1,0:T(8,128)(2,1)}, bf16[2,64,2048]{2,1,0:T(8,128)(2,1)S(1)}, u32[]{:S(2)}, u32[]{:S(2)}) collective-permute-start(bf16[2,64,2048]{2,1,0:T(8,128)(2,1)} %collective-permute-done.48.refs_0_), channel_id=1, source_target_pairs={{0,4},{2,6},{4,0},{6,2},{8,12},{10,14},{12,8},{14,10},{16,20},{18,... | collective-permute-start | bytes 1572872 | tf_op jit(solution)/shard_map/ppermute | solution.py:148
  82.8 24.6 %collective-permute-start.36 = (bf16[2,64,2048]{2,1,0:T(8,128)(2,1)}, bf16[2,64,2048]{2,1,0:T(8,128)(2,1)}, u32[]{:S(2)}, u32[]{:S(2)}) collective-permute-start(bf16[2,64,2048]{2,1,0:T(8,128)(2,1)} %copy-done.24), channel_id=1, source_target_pairs={{0,2},{2,0},{4,6},{6,4},{8,10},{10,8},{12,14},{14,12},{16,18},{18,... | collective-permute-start | bytes 1572872 | tf_op jit(solution)/shard_map/ppermute | solution.py:148
  83.9 25.5 %collective-permute-start.38 = (bf16[2,64,2048]{2,1,0:T(8,128)(2,1)S(1)}, bf16[2,64,2048]{2,1,0:T(8,128)(2,1)}, u32[]{:S(2)}, u32[]{:S(2)}) collective-permute-start(bf16[2,64,2048]{2,1,0:T(8,128)(2,1)S(1)} %collective-permute-done.33.across.refs_2_), channel_id=1, source_target_pairs={{0,2},{2,0},{4,6},{6,4},{8,10},{10,8},{12,14},{14,12},{16,18},{18,... | collective-permute-start | bytes 1572872 | tf_op jit(solution)/shard_map/ppermute | solution.py:148
  83.9 25.5 %collective-permute-start.37 = (bf16[2,64,2048]{2,1,0:T(8,128)(2,1)S(1)}, bf16[2,64,2048]{2,1,0:T(8,128)(2,1)}, u32[]{:S(2)}, u32[]{:S(2)}) collective-permute-start(bf16[2,64,2048]{2,1,0:T(8,128)(2,1)S(1)} %collective-permute-done.32.rest.refs_1_), channel_id=1, source_target_pairs={{0,2},{2,0},{4,6},{6,4},{8,10},{10,8},{12,14},{14,12},{16,18},{18,... | collective-permute-start | bytes 1572872 | tf_op jit(solution)/shard_map/ppermute | solution.py:148
  107.4 15.2 %collective-permute-start.53 = (bf16[2,64,2048]{2,1,0:T(8,128)(2,1)}, bf16[2,64,2048]{2,1,0:T(8,128)(2,1)}, u32[]{:S(2)}, u32[]{:S(2)}) collective-permute-start(bf16[2,64,2048]{2,1,0:T(8,128)(2,1)} %collective-permute-done.48.refs_0_), channel_id=1, source_target_pairs={{0,2},{2,0},{4,6},{6,4},{8,10},{10,8},{12,14},{14,12},{16,18},{18,... | collective-permute-start | bytes 1572872 | tf_op jit(solution)/shard_map/ppermute | solution.py:148
  107.7 15.3 %collective-permute-start.51 = (bf16[64,2048]{1,0:T(8,128)(2,1)S(1)}, bf16[64,2048]{1,0:T(8,128)(2,1)S(1)}, u32[]{:S(2)}, u32[]{:S(2)}) collective-permute-start(bf16[64,2048]{1,0:T(8,128)(2,1)S(1)} %get-tuple-element.108), channel_id=1, source_target_pairs={{0,4},{2,6},{4,0},{6,2},{8,12},{10,14},{12,8},{14,10},{16,20},{18,... | collective-permute-start | bytes 786440 | tf_op jit(solution)/shard_map/ppermute | solution.py:148
  120.8 22.3 %collective-permute-start.41 = (bf16[2,2,2,128,1024]{4,3,2,1,0:T(8,128)(2,1)}, bf16[2,2,2,128,1024]{4,3,2,1,0:T(8,128)(2,1)S(1)}, u32[]{:S(2)}, u32[]{:S(2)}) collective-permute-start(bf16[2,2,2,128,1024]{4,3,2,1,0:T(8,128)(2,1)} %get-tuple-element.100), channel_id=1, source_target_pairs={{0,2},{2,0},{4,6},{6,4},{8,10},{10,8},{12,14},{14,12},{16,18},{18,... | collective-permute-start | bytes 6291464 | tf_op jit(solution)/shard_map/ppermute | solution.py:148
  130.4 19.7 %collective-permute-start.26 = (bf16[2,2,2,128,1024]{4,3,2,1,0:T(8,128)(2,1)}, bf16[2,2,2,128,1024]{4,3,2,1,0:T(8,128)(2,1)}, u32[]{:S(2)}, u32[]{:S(2)}) collective-permute-start(bf16[2,2,2,128,1024]{4,3,2,1,0:T(8,128)(2,1)} %get-tuple-element.86), channel_id=1, source_target_pairs={{0,2},{2,0},{4,6},{6,4},{8,10},{10,8},{12,14},{14,12},{16,18},{18,... | collective-permute-start | bytes 6291464 | tf_op jit(solution)/shard_map/ppermute | solution.py:148
  131.7 35.4 %collective-permute-start.11 = (bf16[2,2,2,128,1024]{4,3,2,1,0:T(8,128)(2,1)}, bf16[2,2,2,128,1024]{4,3,2,1,0:T(8,128)(2,1)}, u32[]{:S(2)}, u32[]{:S(2)}) collective-permute-start(bf16[2,2,2,128,1024]{4,3,2,1,0:T(8,128)(2,1)} %get-tuple-element.71.refs_0_), channel_id=1, source_target_pairs={{0,2},{2,0},{4,6},{6,4},{8,10},{10,8},{12,14},{14,12},{16,18},{18,... | collective-permute-start | bytes 6291464 | tf_op jit(solution)/shard_map/ppermute | solution.py:148
  142.6 28.9 %collective-permute-start.58 = (bf16[2,2,2,128,1024]{4,3,2,1,0:T(8,128)(2,1)}, bf16[2,2,2,128,1024]{4,3,2,1,0:T(8,128)(2,1)}, u32[]{:S(2)}, u32[]{:S(2)}) collective-permute-start(bf16[2,2,2,128,1024]{4,3,2,1,0:T(8,128)(2,1)} %get-tuple-element.116), channel_id=1, source_target_pairs={{0,2},{2,0},{4,6},{6,4},{8,10},{10,8},{12,14},{14,12},{16,18},{18,... | collective-permute-start | bytes 6291464 | tf_op jit(solution)/shard_map/ppermute | solution.py:148
  148.6 15.9 %collective-permute-start.43 = (bf16[2,128,1024]{2,1,0:T(8,128)(2,1)S(1)}, bf16[2,128,1024]{2,1,0:T(8,128)(2,1)S(1)}, u32[]{:S(2)}, u32[]{:S(2)}) collective-permute-start(bf16[2,128,1024]{2,1,0:T(8,128)(2,1)S(1)} %get-tuple-element.103), channel_id=1, source_target_pairs={{0,1},{1,0},{2,3},{3,2},{4,5},{5,4},{6,7},{7,6},{8,9},{9,8},{10,11... | collective-permute-start | bytes 1572872 | tf_op jit(solution)/shard_map/ppermute | solution.py:148
  152.8 22.3 %collective-permute-start.27 = (bf16[2,128,1024]{2,1,0:T(8,128)(2,1)}, bf16[2,128,1024]{2,1,0:T(8,128)(2,1)}, u32[]{:S(2)}, u32[]{:S(2)}) collective-permute-start(bf16[2,128,1024]{2,1,0:T(8,128)(2,1)} %get-tuple-element.88), channel_id=1, source_target_pairs={{0,4},{2,6},{4,0},{6,2},{8,12},{10,14},{12,8},{14,10},{16,20},{18,... | collective-permute-start | bytes 1572872 | tf_op jit(solution)/shard_map/ppermute | solution.py:148
  163.0 15.2 %collective-permute-start.28 = (bf16[2,128,1024]{2,1,0:T(8,128)(2,1)}, bf16[2,128,1024]{2,1,0:T(8,128)(2,1)}, u32[]{:S(2)}, u32[]{:S(2)}) collective-permute-start(bf16[2,128,1024]{2,1,0:T(8,128)(2,1)} %get-tuple-element.89), channel_id=1, source_target_pairs={{0,1},{1,0},{2,3},{3,2},{4,5},{5,4},{6,7},{7,6},{8,9},{9,8},{10,11... | collective-permute-start | bytes 1572872 | tf_op jit(solution)/shard_map/ppermute | solution.py:148
  166.0 17.7 %collective-permute-start.44 = (bf16[128,1024]{1,0:T(8,128)(2,1)}, bf16[128,1024]{1,0:T(8,128)(2,1)S(1)}, u32[]{:S(2)}, u32[]{:S(2)}) collective-permute-start(bf16[128,1024]{1,0:T(8,128)(2,1)} %get-tuple-element.104), channel_id=1, source_target_pairs={{0,1},{1,0},{2,3},{3,2},{4,5},{5,4},{6,7},{7,6},{8,9},{9,8},{10,11... | collective-permute-start | bytes 786440 | tf_op jit(solution)/shard_map/ppermute | solution.py:148
  171.1 37.8 %collective-permute-start.12 = (bf16[2,128,1024]{2,1,0:T(8,128)(2,1)S(1)}, bf16[2,128,1024]{2,1,0:T(8,128)(2,1)S(1)}, u32[]{:S(2)}, u32[]{:S(2)}) collective-permute-start(bf16[2,128,1024]{2,1,0:T(8,128)(2,1)S(1)} %get-tuple-element.73), channel_id=1, source_target_pairs={{0,4},{2,6},{4,0},{6,2},{8,12},{10,14},{12,8},{14,10},{16,20},{18,... | collective-permute-start | bytes 1572872 | tf_op jit(solution)/shard_map/ppermute | solution.py:148
  171.5 39.0 %collective-permute-start.13 = (bf16[2,128,1024]{2,1,0:T(8,128)(2,1)S(1)}, bf16[2,128,1024]{2,1,0:T(8,128)(2,1)S(1)}, u32[]{:S(2)}, u32[]{:S(2)}) collective-permute-start(bf16[2,128,1024]{2,1,0:T(8,128)(2,1)S(1)} %get-tuple-element.74), channel_id=1, source_target_pairs={{0,1},{1,0},{2,3},{3,2},{4,5},{5,4},{6,7},{7,6},{8,9},{9,8},{10,11... | collective-permute-start | bytes 1572872 | tf_op jit(solution)/shard_map/ppermute | solution.py:148
  175.2 16.4 %collective-permute-start.45 = (bf16[128,1024]{1,0:T(8,128)(2,1)S(1)}, bf16[128,1024]{1,0:T(8,128)(2,1)S(1)}, u32[]{:S(2)}, u32[]{:S(2)}) collective-permute-start(bf16[128,1024]{1,0:T(8,128)(2,1)S(1)} %copy-done.17), channel_id=1, source_target_pairs={{0,4},{2,6},{4,0},{6,2},{8,12},{10,14},{12,8},{14,10},{16,20},{18,... | collective-permute-start | bytes 786440 | tf_op jit(solution)/shard_map/ppermute | solution.py:148
  178.2 23.2 %collective-permute-start.59 = (bf16[2,128,1024]{2,1,0:T(8,128)(2,1)S(1)}, bf16[2,128,1024]{2,1,0:T(8,128)(2,1)S(1)}, u32[]{:S(2)}, u32[]{:S(2)}) collective-permute-start(bf16[2,128,1024]{2,1,0:T(8,128)(2,1)S(1)} %get-tuple-element.118), channel_id=1, source_target_pairs={{0,4},{2,6},{4,0},{6,2},{8,12},{10,14},{12,8},{14,10},{16,20},{18,... | collective-permute-start | bytes 1572872 | tf_op jit(solution)/shard_map/ppermute | solution.py:148
  183.7 22.5 %collective-permute-start.60 = (bf16[2,128,1024]{2,1,0:T(8,128)(2,1)S(1)}, bf16[2,128,1024]{2,1,0:T(8,128)(2,1)S(1)}, u32[]{:S(2)}, u32[]{:S(2)}) collective-permute-start(bf16[2,128,1024]{2,1,0:T(8,128)(2,1)S(1)} %get-tuple-element.119), channel_id=1, source_target_pairs={{0,1},{1,0},{2,3},{3,2},{4,5},{5,4},{6,7},{7,6},{8,9},{9,8},{10,11... | collective-permute-start | bytes 1572872 | tf_op jit(solution)/shard_map/ppermute | solution.py:148
  191.6 23.7 %collective-permute-start.29 = (bf16[128,1024]{1,0:T(8,128)(2,1)S(1)}, bf16[128,1024]{1,0:T(8,128)(2,1)S(1)}, u32[]{:S(2)}, u32[]{:S(2)}) collective-permute-start(bf16[128,1024]{1,0:T(8,128)(2,1)S(1)} %get-tuple-element.90), channel_id=1, source_target_pairs={{0,1},{1,0},{2,3},{3,2},{4,5},{5,4},{6,7},{7,6},{8,9},{9,8},{10,11... | collective-permute-start | bytes 786440 | tf_op jit(solution)/shard_map/ppermute | solution.py:148
  222.2 15.8 %collective-permute-start.63 = (bf16[2,128,1024]{2,1,0:T(8,128)(2,1)S(1)}, bf16[2,128,1024]{2,1,0:T(8,128)(2,1)S(1)}, u32[]{:S(2)}, u32[]{:S(2)}) collective-permute-start(bf16[2,128,1024]{2,1,0:T(8,128)(2,1)S(1)} %get-tuple-element.123), channel_id=1, source_target_pairs={{0,8},{2,10},{4,12},{6,14},{8,16},{10,18},{12,20},{14,22},{16,24},... | collective-permute-start | bytes 1572872 | tf_op jit(solution)/shard_map/ppermute | solution.py:153
  (67 other events, 793.8 us)
where the time goes:
time: 243 us; the launch traced here: 239 us
  waiting for transfers between devices  93 us (38%)
  Pallas kernels  60.6 us (25%)
  starting transfers between devices  48.9 us (20%)
  local copies, waits for them, and re-layouts  19.3 us (8%)
  matrix products  11.5 us (5%)
  other arithmetic  4.14 us (2%)
    pallas_call x20, Pallas kernels, call_kernel(): pl.pallas_call(kernel, out_shape=shapes, in_specs=options.pop('in_specs',...  60.6 us
    ppermute x55, waiting for transfers between devices, swap(): return lax.ppermute(values, axis_name, [(i, i ^ bit) for i in range(size)])  54.5 us
    ppermute x55, starting transfers between devices, swap(): return lax.ppermute(values, axis_name, [(i, i ^ bit) for i in range(size)])  39.6 us
    ppermute x9, waiting for transfers between devices, shift(): lax.ppermute(values, 'dp', [(i, (i + 4 * steps) % size) for i in range(si...  38.5 us
    unnamed x70, local copies, waits for them, and re-layouts  12.7 us
    dot_general x3, matrix products, mxu(): lax.dot_general(a, b, (dims, ((), ())), preferred_element_type=jnp.float32)  11.3 us
    ppermute x9, starting transfers between devices, shift(): lax.ppermute(values, 'dp', [(i, (i + 4 * steps) % size) for i in range(si...  9.32 us
  transfers between devices with their start and end apart: 64, of which 21 were waited for; matrix products, arithmetic and copies ran while one was open for 8% of the time, Pallas kernels for 25%

commit v1 on v0

--- a/solution.py
+++ b/solution.py
@@ -153,14 +153,20 @@
     return lax.ppermute(values, "dp", [(i, (i + 4 * steps) % size) for i in range(size)])
 
 
-def cut_halves(part_ref, tokens, cots, table, mine, other, table_out):
-    table_out[...] = table[...]
+def cut_halves(part_ref, tokens, cots, table, mine, other, table_out, sems):
     rows = tokens.shape[0] // 2
     own = pl.multiple_of(part_ref[0] * rows, rows)
     rest = pl.multiple_of(rows - part_ref[0] * rows, rows)
+    copies = []
     for kind, values in enumerate((tokens, cots)):
-        mine[kind] = values[pl.ds(own, rows), :]
-        other[kind] = values[pl.ds(rest, rows), :]
+        for i, (start, out) in enumerate(((own, mine), (rest, other))):
+            source = values.at[pl.ds(start, rows)]
+            copies.append(pltpu.make_async_copy(source, out.at[kind], sems.at[kind, i]))
+    for copy in copies:
+        copy.start()
+    table_out[...] = table[...]
+    for copy in copies:
+        copy.wait()
 
 
 def own_halves(part_arg, tokens, cots, table):
@@ -171,7 +177,8 @@
         "own_halves",
         [shape, shape, jax.ShapeDtypeStruct(table.shape, table.dtype)],
         [part_arg, tokens, cots, table],
-        in_specs=[pl.BlockSpec(memory_space=pltpu.SMEM), vmem, vmem, vmem],
+        in_specs=[pl.BlockSpec(memory_space=pltpu.SMEM)] + [pl.BlockSpec(memory_space=pl.ANY)] * 2 + [vmem],
+        scratch_shapes=[pltpu.SemaphoreType.DMA((2, 2))],
     )
 
 

time: 243 us -> 243 us (level)
  no operation moved by 1% of the time
where the time goes in v1:
time: 243 us; the launch traced here: 240 us
  waiting for transfers between devices  93 us (38%)
  Pallas kernels  60.6 us (25%)
  starting transfers between devices  48.9 us (20%)
  local copies, waits for them, and re-layouts  19.3 us (8%)
  matrix products  11.5 us (5%)
  other arithmetic  4.14 us (2%)
    pallas_call x20, Pallas kernels, call_kernel(): pl.pallas_call(kernel, out_shape=shapes, in_specs=options.pop('in_specs',...  60.6 us
    ppermute x55, waiting for transfers between devices, swap(): return lax.ppermute(values, axis_name, [(i, i ^ bit) for i in range(size)])  54.5 us
    ppermute x55, starting transfers between devices, swap(): return lax.ppermute(values, axis_name, [(i, i ^ bit) for i in range(size)])  39.6 us
    ppermute x9, waiting for transfers between devices, shift(): lax.ppermute(values, 'dp', [(i, (i + 4 * steps) % size) for i in range(si...  38.5 us
    unnamed x70, local copies, waits for them, and re-layouts  12.7 us
    dot_general x3, matrix products, mxu(): lax.dot_general(a, b, (dims, ((), ())), preferred_element_type=jnp.float32)  11.3 us
    ppermute x9, starting transfers between devices, shift(): lax.ppermute(values, 'dp', [(i, (i + 4 * steps) % size) for i in range(si...  9.32 us
  transfers between devices with their start and end apart: 64, of which 21 were waited for; matrix products, arithmetic and copies ran while one was open for 8% of the time, Pallas kernels for 25%

profile of v1, /device:TPU:0, one launch (start us, length us, event | category | flops | bytes accessed | tf_op | source)
XLA Modules:
  0.0 239.5 jit_solution(18067378442889028281)
XLA Ops:
  4.3 3.1 %collective-permute-start.16 = (bf16[2,64,2048]{2,1,0:T(8,128)(2,1)S(1)}, bf16[2,64,2048]{2,1,0:T(8,128)(2,1)S(1)}, u32[]{:S(2)}, u32[]{:S(2)}) collective-permute-start(bf16[2,64,2048]{2,1,0:T(8,128)(2,1)S(1)} %get-tuple-element.68.refs_0_), channel_id=1, source_target_pairs={{0,8},{2,10},{4,12},{6,14},{8,16},{10,18},{12,20},{14,22},{16,24},... | collective-permute-start | bytes 1572872 | tf_op jit(solution)/shard_map/ppermute | solution.py:153
  8.8 12.5 %collective-permute-done.16.refs_0_ = bf16[2,64,2048]{2,1,0:T(8,128)(2,1)S(1)} collective-permute-done((bf16[2,64,2048]{2,1,0:T(8,128)(2,1)S(1)}, bf16[2,64,2048]{2,1,0:T(8,128)(2,1)S(1)}, u32[]{:S(2)}, u32[]{:S(2)}) %collective-permute-start.16) | collective-permute-done | bytes 524320 | tf_op jit(solution)/shard_map/ppermute | solution.py:153
  24.5 2.0 collective-permute-done.2
  26.5 2.6 %collective-permute-done.1 = f32[24,128]{1,0:T(8,128)S(1)} collective-permute-done((f32[24,128]{1,0:T(8,128)S(1)}, f32[24,128]{1,0:T(8,128)S(1)}, u32[]{:S(2)}, u32[]{:S(2)}) %collective-permute-start.1) | collective-permute-done | bytes 12320 | tf_op jit(solution)/shard_map/ppermute | solution.py:153
  29.1 2.9 %collective-permute-done = f32[24,128]{1,0:T(8,128)S(1)} collective-permute-done((f32[24,128]{1,0:T(8,128)S(1)}, f32[24,128]{1,0:T(8,128)S(1)}, u32[]{:S(2)}, u32[]{:S(2)}) %collective-permute-start) | collective-permute-done | bytes 12320 | tf_op jit(solution)/shard_map/ppermute | solution.py:153
  34.1 2.0 collective-permute-done.3
  40.6 2.3 collective-permute-done.17.rest.refs_1_
  46.4 7.3 %collective-permute-done.31.refs_0_ = bf16[2,64,2048]{2,1,0:T(8,128)(2,1)S(1)} collective-permute-done((bf16[2,64,2048]{2,1,0:T(8,128)(2,1)S(1)}, bf16[2,64,2048]{2,1,0:T(8,128)(2,1)S(1)}, u32[]{:S(2)}, u32[]{:S(2)}) %collective-permute-start.31) | collective-permute-done | bytes 524320 | tf_op jit(solution)/shard_map/ppermute | solution.py:153
  58.1 5.0 %collective-permute-done.20.refs_4_ = bf16[64,2048]{1,0:T(8,128)(2,1)} collective-permute-done((bf16[64,2048]{1,0:T(8,128)(2,1)S(1)}, bf16[64,2048]{1,0:T(8,128)(2,1)}, u32[]{:S(2)}, u32[]{:S(2)}) %collective-permute-start.20) | collective-permute-done | bytes 262176 | tf_op jit(solution)/shard_map/ppermute | solution.py:148
  63.9 4.5 %collective-permute-done.33.across.refs_2_ = bf16[2,64,2048]{2,1,0:T(8,128)(2,1)S(1)} collective-permute-done((bf16[2,64,2048]{2,1,0:T(8,128)(2,1)S(1)}, bf16[2,64,2048]{2,1,0:T(8,128)(2,1)S(1)}, u32[]{:S(2)}, u32[]{:S(2)}) %collective-permute-start.33) | collective-permute-done | bytes 524320 | tf_op jit(solution)/shard_map/ppermute | solution.py:148
  69.3 3.4 %collective-permute-done.32.rest.refs_1_ = bf16[2,64,2048]{2,1,0:T(8,128)(2,1)S(1)} collective-permute-done((bf16[2,64,2048]{2,1,0:T(8,128)(2,1)S(1)}, bf16[2,64,2048]{2,1,0:T(8,128)(2,1)S(1)}, u32[]{:S(2)}, u32[]{:S(2)}) %collective-permute-start.32) | collective-permute-done | bytes 524320 | tf_op jit(solution)/shard_map/ppermute | solution.py:148
  84.4 10.7 %chunk.4 = (bf16[2,2,2,128,1024]{4,3,2,1,0:T(8,128)(2,1)}, bf16[2,2,2,128,1024]{4,3,2,1,0:T(8,128)(2,1)}, bf16[1024,2048]{1,0:T(8,128)(2,1)}, bf16[1024,2048]{1,...) custom-call(s32[1]{0:T(128)} %bitcast.part_ref, ...), custom_call_target="tpu_custom_call" | custom-call | flops 3221225472 | bytes 26346500 | tf_op jit(solution)/shard_map/chunk/pallas_call | solution.py:270
  95.8 10.7 %chunk.5 = (bf16[2,2,2,128,1024]{4,3,2,1,0:T(8,128)(2,1)}, bf16[2,2,2,128,1024]{4,3,2,1,0:T(8,128)(2,1)}, bf16[1024,2048]{1,0:T(8,128)(2,1)}, bf16[1024,2048]{1,...) custom-call(s32[1]{0:T(128)} %bitcast.part_ref, ...), custom_call_target="tpu_custom_call", output_to_operand_aliasing={{2}: (17, {}), {3}: (18, {}), {4}: (19, {}), {5}: (20, {}),... | custom-call | flops 3221225472 | bytes 37880836 | tf_op jit(solution)/shard_map/chunk/pallas_call | solution.py:270
  110.1 10.8 %chunk.6 = (bf16[2,2,2,128,1024]{4,3,2,1,0:T(8,128)(2,1)}, bf16[2,2,2,128,1024]{4,3,2,1,0:T(8,128)(2,1)}, bf16[1024,2048]{1,0:T(8,128)(2,1)}, bf16[1024,2048]{1,...) custom-call(s32[1]{0:T(128)} %bitcast.part_ref, ...), custom_call_target="tpu_custom_call", output_to_operand_aliasing={{2}: (17, {}), {3}: (18, {}), {4}: (19, {}), {5}: (20, {}),... | custom-call | flops 3221225472 | bytes 37880836 | tf_op jit(solution)/shard_map/chunk/pallas_call | solution.py:270
  123.2 6.6 %collective-permute-done.52.refs_4_ = bf16[64,2048]{1,0:T(8,128)(2,1)} collective-permute-done((bf16[64,2048]{1,0:T(8,128)(2,1)S(1)}, bf16[64,2048]{1,0:T(8,128)(2,1)}, u32[]{:S(2)}, u32[]{:S(2)}) %collective-permute-start.52) | collective-permute-done | bytes 262176 | tf_op jit(solution)/shard_map/ppermute | solution.py:148
  131.8 10.8 %chunk.7 = (bf16[2,2,2,128,1024]{4,3,2,1,0:T(8,128)(2,1)}, bf16[2,2,2,128,1024]{4,3,2,1,0:T(8,128)(2,1)}, bf16[1024,2048]{1,0:T(8,128)(2,1)}, bf16[1024,2048]{1,...) custom-call(s32[1]{0:T(128)} %bitcast.part_ref, ...), custom_call_target="tpu_custom_call", output_to_operand_aliasing={{2}: (17, {}), {3}: (18, {}), {4}: (19, {}), {5}: (20, {}),... | custom-call | flops 3221225472 | bytes 37880836 | tf_op jit(solution)/shard_map/chunk/pallas_call | solution.py:270
  150.2 2.7 %add_cores.5 = (bf16[2,128,1024]{2,1,0:T(8,128)(2,1)}, bf16[2,128,1024]{2,1,0:T(8,128)(2,1)}, bf16[2,2,128,1024]{3,2,1,0:T(8,128)(2,1)S(1)}, f32[8,128]{1,0:T(8,128)}) custom-call(bf16[2,2,2,128,1024]{4,3,2,1,0:T(8,128)(2,1)S(1)} %copy-done.5, bf16[2,2,2,128,1024]{4,3,2,1,0:T(8,128)(2,1)} %collective-permute-done.26.got), custom_call_target="tpu_custom_call" | custom-call | bytes 6295552 | tf_op jit(solution)/shard_map/add_cores/pallas_call | solution.py:270
  154.5 8.5 %collective-permute-done.42.away_out = bf16[2,128,1024]{2,1,0:T(8,128)(2,1)S(1)} collective-permute-done((bf16[2,128,1024]{2,1,0:T(8,128)(2,1)S(1)}, bf16[2,128,1024]{2,1,0:T(8,128)(2,1)S(1)}, u32[]{:S(2)}, u32[]{:S(2)}) %collective-permute-start.42) | collective-permute-done | bytes 524320 | tf_op jit(solution)/shard_map/ppermute | solution.py:148
  168.8 2.3 add_cores.4
  173.0 2.2 add_cores.7
  178.6 5.2 %collective-permute-done.44.last_out = bf16[128,1024]{1,0:T(8,128)(2,1)S(1)} collective-permute-done((bf16[128,1024]{1,0:T(8,128)(2,1)}, bf16[128,1024]{1,0:T(8,128)(2,1)S(1)}, u32[]{:S(2)}, u32[]{:S(2)}) %collective-permute-start.44) | collective-permute-done | bytes 262176 | tf_op jit(solution)/shard_map/ppermute | solution.py:148
  185.3 3.8 %fusion = bf16[1,2048,512]{2,1,0:T(8,128)(2,1)} fusion(bf16[1024,2048]{1,0:T(8,128)(2,1)S(1)} %copy-done.18, bf16[1024,512]{1,0:T(8,128)(2,1)S(1)} %copy-done.21, f32[]{:T(128)S(6)} %div.3), kind=kOutput, calls=%fused_computation.3 | convolution fusion | flops 2149580800 | bytes 7340036 | tf_op jit(solution)/shard_map/dot_general | solution.py:237
  189.1 1.9 add_first.5
  193.3 8.1 %collective-permute-done.59.away_out = bf16[2,128,1024]{2,1,0:T(8,128)(2,1)S(1)} collective-permute-done((bf16[2,128,1024]{2,1,0:T(8,128)(2,1)S(1)}, bf16[2,128,1024]{2,1,0:T(8,128)(2,1)S(1)}, u32[]{:S(2)}, u32[]{:S(2)}) %collective-permute-start.59) | collective-permute-done | bytes 524320 | tf_op jit(solution)/shard_map/ppermute | solution.py:148
  201.8 4.4 %collective-permute-done.60.away_grad = bf16[2,128,1024]{2,1,0:T(8,128)(2,1)S(1)} collective-permute-done((bf16[2,128,1024]{2,1,0:T(8,128)(2,1)S(1)}, bf16[2,128,1024]{2,1,0:T(8,128)(2,1)S(1)}, u32[]{:S(2)}, u32[]{:S(2)}) %collective-permute-start.60) | collective-permute-done | bytes 524320 | tf_op jit(solution)/shard_map/ppermute | solution.py:148
  206.2 2.1 collective-permute-start.46
  210.8 3.8 %fusion.1 = bf16[1,2048,512]{2,1,0:T(8,128)(2,1)} fusion(bf16[1024,2048]{1,0:T(8,128)(2,1)S(1)} %copy-done.18, bf16[1024,512]{1,0:T(8,128)(2,1)S(1)} %copy-done.22, f32[]{:T(128)S(6)} %div.3), kind=kOutput, calls=%fused_computation.4 | convolution fusion | flops 2149580800 | bytes 7340036 | tf_op jit(solution)/shard_map/dot_general | solution.py:237
  217.4 1.8 add_last.6
  219.2 2.4 collective-permute-start.47
  222.3 3.8 %fusion.2 = bf16[1,512,2048]{2,1,0:T(8,128)(2,1)} fusion(bf16[1024,512]{1,0:T(8,128)(2,1)S(1)} %copy-done.20, bf16[1024,2048]{1,0:T(8,128)(2,1)S(1)} %copy-done.19, f32[]{:T(128)S(6)} %div.3), kind=kOutput, calls=%fused_computation.5 | convolution fusion | flops 2149580800 | bytes 7340036 | tf_op jit(solution)/shard_map/dot_general | solution.py:237
  226.7 5.7 %collective-permute-done.47 = bf16[2,128,1024]{2,1,0:T(8,128)(2,1)S(1)} collective-permute-done((bf16[2,128,1024]{2,1,0:T(8,128)(2,1)S(1)}, bf16[2,128,1024]{2,1,0:T(8,128)(2,1)S(1)}, u32[]{:S(2)}, u32[]{:S(2)}) %collective-permute-start.47) | collective-permute-done | bytes 524320 | tf_op jit(solution)/shard_map/ppermute | solution.py:153
  232.4 5.6 %collective-permute-done.63 = bf16[2,128,1024]{2,1,0:T(8,128)(2,1)S(1)} collective-permute-done((bf16[2,128,1024]{2,1,0:T(8,128)(2,1)S(1)}, bf16[2,128,1024]{2,1,0:T(8,128)(2,1)S(1)}, u32[]{:S(2)}, u32[]{:S(2)}) %collective-permute-start.63) | collective-permute-done | bytes 524320 | tf_op jit(solution)/shard_map/ppermute | solution.py:153
  (212 shorter events, 76.2 us)
Async XLA Ops:
  4.3 17.0 %collective-permute-start.16 = (bf16[2,64,2048]{2,1,0:T(8,128)(2,1)S(1)}, bf16[2,64,2048]{2,1,0:T(8,128)(2,1)S(1)}, u32[]{:S(2)}, u32[]{:S(2)}) collective-permute-start(bf16[2,64,2048]{2,1,0:T(8,128)(2,1)S(1)} %get-tuple-element.68.refs_0_), channel_id=1, source_target_pairs={{0,8},{2,10},{4,12},{6,14},{8,16},{10,18},{12,20},{14,22},{16,24},... | collective-permute-start | bytes 1572872 | tf_op jit(solution)/shard_map/ppermute | solution.py:153
  7.3 30.4 %collective-permute-start.8 = (bf16[2,64,2048]{2,1,0:T(8,128)(2,1)S(1)}, bf16[2,64,2048]{2,1,0:T(8,128)(2,1)S(1)}, u32[]{:S(2)}, u32[]{:S(2)}) collective-permute-start(bf16[2,64,2048]{2,1,0:T(8,128)(2,1)S(1)} %get-tuple-element.69.refs_1_), channel_id=1, source_target_pairs={{0,2},{2,0},{4,6},{6,4},{8,10},{10,8},{12,14},{14,12},{16,18},{18,... | collective-permute-start | bytes 1572872 | tf_op jit(solution)/shard_map/ppermute | solution.py:148
  7.3 30.4 %collective-permute-start.5 = (bf16[2,64,2048]{2,1,0:T(8,128)(2,1)S(1)}, bf16[2,64,2048]{2,1,0:T(8,128)(2,1)S(1)}, u32[]{:S(2)}, u32[]{:S(2)}) collective-permute-start(bf16[2,64,2048]{2,1,0:T(8,128)(2,1)S(1)} %get-tuple-element.68.refs_0_), channel_id=1, source_target_pairs={{0,4},{2,6},{4,0},{6,2},{8,12},{10,14},{12,8},{14,10},{16,20},{18,... | collective-permute-start | bytes 1572872 | tf_op jit(solution)/shard_map/ppermute | solution.py:148
  21.3 19.0 %collective-permute-start.18 = (bf16[2,64,2048]{2,1,0:T(8,128)(2,1)S(1)}, bf16[2,64,2048]{2,1,0:T(8,128)(2,1)S(1)}, u32[]{:S(2)}, u32[]{:S(2)}) collective-permute-start(bf16[2,64,2048]{2,1,0:T(8,128)(2,1)S(1)} %collective-permute-done.16.refs_0_), channel_id=1, source_target_pairs={{0,4},{2,6},{4,0},{6,2},{8,12},{10,14},{12,8},{14,10},{16,20},{18,... | collective-permute-start | bytes 1572872 | tf_op jit(solution)/shard_map/ppermute | solution.py:148
  37.7 16.0 %collective-permute-start.31 = (bf16[2,64,2048]{2,1,0:T(8,128)(2,1)S(1)}, bf16[2,64,2048]{2,1,0:T(8,128)(2,1)S(1)}, u32[]{:S(2)}, u32[]{:S(2)}) collective-permute-start(bf16[2,64,2048]{2,1,0:T(8,128)(2,1)S(1)} %collective-permute-done.16.refs_0_), channel_id=1, source_target_pairs={{0,8},{2,10},{4,12},{6,14},{8,16},{10,18},{12,20},{14,22},{16,24},... | collective-permute-start | bytes 1572872 | tf_op jit(solution)/shard_map/ppermute | solution.py:153
  39.3 15.9 %collective-permute-start.21 = (bf16[2,64,2048]{2,1,0:T(8,128)(2,1)S(1)}, bf16[2,64,2048]{2,1,0:T(8,128)(2,1)S(1)}, u32[]{:S(2)}, u32[]{:S(2)}) collective-permute-start(bf16[2,64,2048]{2,1,0:T(8,128)(2,1)S(1)} %collective-permute-done.16.refs_0_), channel_id=1, source_target_pairs={{0,2},{2,0},{4,6},{6,4},{8,10},{10,8},{12,14},{14,12},{16,18},{18,... | collective-permute-start | bytes 1572872 | tf_op jit(solution)/shard_map/ppermute | solution.py:148
  40.3 15.7 %collective-permute-start.9 = (bf16[2,64,2048]{2,1,0:T(8,128)(2,1)}, bf16[2,64,2048]{2,1,0:T(8,128)(2,1)S(1)}, u32[]{:S(2)}, u32[]{:S(2)}) collective-permute-start(bf16[2,64,2048]{2,1,0:T(8,128)(2,1)} %copy-done.33), channel_id=1, source_target_pairs={{0,2},{2,0},{4,6},{6,4},{8,10},{10,8},{12,14},{14,12},{16,18},{18,... | collective-permute-start | bytes 1572872 | tf_op jit(solution)/shard_map/ppermute | solution.py:148
  43.0 14.9 %collective-permute-start.6 = (bf16[2,64,2048]{2,1,0:T(8,128)(2,1)}, bf16[2,64,2048]{2,1,0:T(8,128)(2,1)}, u32[]{:S(2)}, u32[]{:S(2)}) collective-permute-start(bf16[2,64,2048]{2,1,0:T(8,128)(2,1)} %copy-done.33), channel_id=1, source_target_pairs={{0,1},{1,0},{2,3},{3,2},{4,5},{5,4},{6,7},{7,6},{8,9},{9,8},{10,11... | collective-permute-start | bytes 1572872 | tf_op jit(solution)/shard_map/ppermute | solution.py:148
  56.8 15.9 %collective-permute-start.32 = (bf16[2,64,2048]{2,1,0:T(8,128)(2,1)S(1)}, bf16[2,64,2048]{2,1,0:T(8,128)(2,1)S(1)}, u32[]{:S(2)}, u32[]{:S(2)}) collective-permute-start(bf16[2,64,2048]{2,1,0:T(8,128)(2,1)S(1)} %collective-permute-done.31.refs_0_), channel_id=1, source_target_pairs={{0,1},{1,0},{2,3},{3,2},{4,5},{5,4},{6,7},{7,6},{8,9},{9,8},{10,11... | collective-permute-start | bytes 1572872 | tf_op jit(solution)/shard_map/ppermute | solution.py:148
  57.9 15.9 %collective-permute-start.48 = (bf16[2,64,2048]{2,1,0:T(8,128)(2,1)S(1)}, bf16[2,64,2048]{2,1,0:T(8,128)(2,1)}, u32[]{:S(2)}, u32[]{:S(2)}) collective-permute-start(bf16[2,64,2048]{2,1,0:T(8,128)(2,1)S(1)} %collective-permute-done.31.refs_0_), channel_id=1, source_target_pairs={{0,8},{2,10},{4,12},{6,14},{8,16},{10,18},{12,20},{14,22},{16,24},... | collective-permute-start | bytes 1572872 | tf_op jit(solution)/shard_map/ppermute | solution.py:153
  58.0 16.4 %collective-permute-start.23 = (bf16[2,64,2048]{2,1,0:T(8,128)(2,1)S(1)}, bf16[2,64,2048]{2,1,0:T(8,128)(2,1)S(1)}, u32[]{:S(2)}, u32[]{:S(2)}) collective-permute-start(bf16[2,64,2048]{2,1,0:T(8,128)(2,1)S(1)} %collective-permute-done.18.across.refs_2_), channel_id=1, source_target_pairs={{0,2},{2,0},{4,6},{6,4},{8,10},{10,8},{12,14},{14,12},{16,18},{18,... | collective-permute-start | bytes 1572872 | tf_op jit(solution)/shard_map/ppermute | solution.py:148
  78.9 16.3 %collective-permute-start.50 = (bf16[2,64,2048]{2,1,0:T(8,128)(2,1)}, bf16[2,64,2048]{2,1,0:T(8,128)(2,1)S(1)}, u32[]{:S(2)}, u32[]{:S(2)}) collective-permute-start(bf16[2,64,2048]{2,1,0:T(8,128)(2,1)} %collective-permute-done.48.refs_0_), channel_id=1, source_target_pairs={{0,4},{2,6},{4,0},{6,2},{8,12},{10,14},{12,8},{14,10},{16,20},{18,... | collective-permute-start | bytes 1572872 | tf_op jit(solution)/shard_map/ppermute | solution.py:148
  82.8 24.6 %collective-permute-start.36 = (bf16[2,64,2048]{2,1,0:T(8,128)(2,1)}, bf16[2,64,2048]{2,1,0:T(8,128)(2,1)}, u32[]{:S(2)}, u32[]{:S(2)}) collective-permute-start(bf16[2,64,2048]{2,1,0:T(8,128)(2,1)} %copy-done.24), channel_id=1, source_target_pairs={{0,2},{2,0},{4,6},{6,4},{8,10},{10,8},{12,14},{14,12},{16,18},{18,... | collective-permute-start | bytes 1572872 | tf_op jit(solution)/shard_map/ppermute | solution.py:148
  83.9 25.5 %collective-permute-start.38 = (bf16[2,64,2048]{2,1,0:T(8,128)(2,1)S(1)}, bf16[2,64,2048]{2,1,0:T(8,128)(2,1)}, u32[]{:S(2)}, u32[]{:S(2)}) collective-permute-start(bf16[2,64,2048]{2,1,0:T(8,128)(2,1)S(1)} %collective-permute-done.33.across.refs_2_), channel_id=1, source_target_pairs={{0,2},{2,0},{4,6},{6,4},{8,10},{10,8},{12,14},{14,12},{16,18},{18,... | collective-permute-start | bytes 1572872 | tf_op jit(solution)/shard_map/ppermute | solution.py:148
  83.9 25.5 %collective-permute-start.37 = (bf16[2,64,2048]{2,1,0:T(8,128)(2,1)S(1)}, bf16[2,64,2048]{2,1,0:T(8,128)(2,1)}, u32[]{:S(2)}, u32[]{:S(2)}) collective-permute-start(bf16[2,64,2048]{2,1,0:T(8,128)(2,1)S(1)} %collective-permute-done.32.rest.refs_1_), channel_id=1, source_target_pairs={{0,2},{2,0},{4,6},{6,4},{8,10},{10,8},{12,14},{14,12},{16,18},{18,... | collective-permute-start | bytes 1572872 | tf_op jit(solution)/shard_map/ppermute | solution.py:148
  107.4 15.3 %collective-permute-start.53 = (bf16[2,64,2048]{2,1,0:T(8,128)(2,1)}, bf16[2,64,2048]{2,1,0:T(8,128)(2,1)}, u32[]{:S(2)}, u32[]{:S(2)}) collective-permute-start(bf16[2,64,2048]{2,1,0:T(8,128)(2,1)} %collective-permute-done.48.refs_0_), channel_id=1, source_target_pairs={{0,2},{2,0},{4,6},{6,4},{8,10},{10,8},{12,14},{14,12},{16,18},{18,... | collective-permute-start | bytes 1572872 | tf_op jit(solution)/shard_map/ppermute | solution.py:148
  107.7 15.3 %collective-permute-start.51 = (bf16[64,2048]{1,0:T(8,128)(2,1)S(1)}, bf16[64,2048]{1,0:T(8,128)(2,1)S(1)}, u32[]{:S(2)}, u32[]{:S(2)}) collective-permute-start(bf16[64,2048]{1,0:T(8,128)(2,1)S(1)} %get-tuple-element.108), channel_id=1, source_target_pairs={{0,4},{2,6},{4,0},{6,2},{8,12},{10,14},{12,8},{14,10},{16,20},{18,... | collective-permute-start | bytes 786440 | tf_op jit(solution)/shard_map/ppermute | solution.py:148
  120.9 22.3 %collective-permute-start.41 = (bf16[2,2,2,128,1024]{4,3,2,1,0:T(8,128)(2,1)}, bf16[2,2,2,128,1024]{4,3,2,1,0:T(8,128)(2,1)S(1)}, u32[]{:S(2)}, u32[]{:S(2)}) collective-permute-start(bf16[2,2,2,128,1024]{4,3,2,1,0:T(8,128)(2,1)} %get-tuple-element.100), channel_id=1, source_target_pairs={{0,2},{2,0},{4,6},{6,4},{8,10},{10,8},{12,14},{14,12},{16,18},{18,... | collective-permute-start | bytes 6291464 | tf_op jit(solution)/shard_map/ppermute | solution.py:148
  130.5 19.7 %collective-permute-start.26 = (bf16[2,2,2,128,1024]{4,3,2,1,0:T(8,128)(2,1)}, bf16[2,2,2,128,1024]{4,3,2,1,0:T(8,128)(2,1)}, u32[]{:S(2)}, u32[]{:S(2)}) collective-permute-start(bf16[2,2,2,128,1024]{4,3,2,1,0:T(8,128)(2,1)} %get-tuple-element.86), channel_id=1, source_target_pairs={{0,2},{2,0},{4,6},{6,4},{8,10},{10,8},{12,14},{14,12},{16,18},{18,... | collective-permute-start | bytes 6291464 | tf_op jit(solution)/shard_map/ppermute | solution.py:148
  131.8 35.4 %collective-permute-start.11 = (bf16[2,2,2,128,1024]{4,3,2,1,0:T(8,128)(2,1)}, bf16[2,2,2,128,1024]{4,3,2,1,0:T(8,128)(2,1)}, u32[]{:S(2)}, u32[]{:S(2)}) collective-permute-start(bf16[2,2,2,128,1024]{4,3,2,1,0:T(8,128)(2,1)} %get-tuple-element.71.refs_0_), channel_id=1, source_target_pairs={{0,2},{2,0},{4,6},{6,4},{8,10},{10,8},{12,14},{14,12},{16,18},{18,... | collective-permute-start | bytes 6291464 | tf_op jit(solution)/shard_map/ppermute | solution.py:148
  142.6 28.9 %collective-permute-start.58 = (bf16[2,2,2,128,1024]{4,3,2,1,0:T(8,128)(2,1)}, bf16[2,2,2,128,1024]{4,3,2,1,0:T(8,128)(2,1)}, u32[]{:S(2)}, u32[]{:S(2)}) collective-permute-start(bf16[2,2,2,128,1024]{4,3,2,1,0:T(8,128)(2,1)} %get-tuple-element.116), channel_id=1, source_target_pairs={{0,2},{2,0},{4,6},{6,4},{8,10},{10,8},{12,14},{14,12},{16,18},{18,... | collective-permute-start | bytes 6291464 | tf_op jit(solution)/shard_map/ppermute | solution.py:148
  148.7 15.9 %collective-permute-start.43 = (bf16[2,128,1024]{2,1,0:T(8,128)(2,1)S(1)}, bf16[2,128,1024]{2,1,0:T(8,128)(2,1)S(1)}, u32[]{:S(2)}, u32[]{:S(2)}) collective-permute-start(bf16[2,128,1024]{2,1,0:T(8,128)(2,1)S(1)} %get-tuple-element.103), channel_id=1, source_target_pairs={{0,1},{1,0},{2,3},{3,2},{4,5},{5,4},{6,7},{7,6},{8,9},{9,8},{10,11... | collective-permute-start | bytes 1572872 | tf_op jit(solution)/shard_map/ppermute | solution.py:148
  152.9 22.3 %collective-permute-start.27 = (bf16[2,128,1024]{2,1,0:T(8,128)(2,1)}, bf16[2,128,1024]{2,1,0:T(8,128)(2,1)}, u32[]{:S(2)}, u32[]{:S(2)}) collective-permute-start(bf16[2,128,1024]{2,1,0:T(8,128)(2,1)} %get-tuple-element.88), channel_id=1, source_target_pairs={{0,4},{2,6},{4,0},{6,2},{8,12},{10,14},{12,8},{14,10},{16,20},{18,... | collective-permute-start | bytes 1572872 | tf_op jit(solution)/shard_map/ppermute | solution.py:148
  163.1 15.2 %collective-permute-start.28 = (bf16[2,128,1024]{2,1,0:T(8,128)(2,1)}, bf16[2,128,1024]{2,1,0:T(8,128)(2,1)}, u32[]{:S(2)}, u32[]{:S(2)}) collective-permute-start(bf16[2,128,1024]{2,1,0:T(8,128)(2,1)} %get-tuple-element.89), channel_id=1, source_target_pairs={{0,1},{1,0},{2,3},{3,2},{4,5},{5,4},{6,7},{7,6},{8,9},{9,8},{10,11... | collective-permute-start | bytes 1572872 | tf_op jit(solution)/shard_map/ppermute | solution.py:148
  166.1 17.7 %collective-permute-start.44 = (bf16[128,1024]{1,0:T(8,128)(2,1)}, bf16[128,1024]{1,0:T(8,128)(2,1)S(1)}, u32[]{:S(2)}, u32[]{:S(2)}) collective-permute-start(bf16[128,1024]{1,0:T(8,128)(2,1)} %get-tuple-element.104), channel_id=1, source_target_pairs={{0,1},{1,0},{2,3},{3,2},{4,5},{5,4},{6,7},{7,6},{8,9},{9,8},{10,11... | collective-permute-start | bytes 786440 | tf_op jit(solution)/shard_map/ppermute | solution.py:148
  171.1 37.8 %collective-permute-start.12 = (bf16[2,128,1024]{2,1,0:T(8,128)(2,1)S(1)}, bf16[2,128,1024]{2,1,0:T(8,128)(2,1)S(1)}, u32[]{:S(2)}, u32[]{:S(2)}) collective-permute-start(bf16[2,128,1024]{2,1,0:T(8,128)(2,1)S(1)} %get-tuple-element.73), channel_id=1, source_target_pairs={{0,4},{2,6},{4,0},{6,2},{8,12},{10,14},{12,8},{14,10},{16,20},{18,... | collective-permute-start | bytes 1572872 | tf_op jit(solution)/shard_map/ppermute | solution.py:148
  171.5 39.0 %collective-permute-start.13 = (bf16[2,128,1024]{2,1,0:T(8,128)(2,1)S(1)}, bf16[2,128,1024]{2,1,0:T(8,128)(2,1)S(1)}, u32[]{:S(2)}, u32[]{:S(2)}) collective-permute-start(bf16[2,128,1024]{2,1,0:T(8,128)(2,1)S(1)} %get-tuple-element.74), channel_id=1, source_target_pairs={{0,1},{1,0},{2,3},{3,2},{4,5},{5,4},{6,7},{7,6},{8,9},{9,8},{10,11... | collective-permute-start | bytes 1572872 | tf_op jit(solution)/shard_map/ppermute | solution.py:148
  175.2 16.4 %collective-permute-start.45 = (bf16[128,1024]{1,0:T(8,128)(2,1)S(1)}, bf16[128,1024]{1,0:T(8,128)(2,1)S(1)}, u32[]{:S(2)}, u32[]{:S(2)}) collective-permute-start(bf16[128,1024]{1,0:T(8,128)(2,1)S(1)} %copy-done.17), channel_id=1, source_target_pairs={{0,4},{2,6},{4,0},{6,2},{8,12},{10,14},{12,8},{14,10},{16,20},{18,... | collective-permute-start | bytes 786440 | tf_op jit(solution)/shard_map/ppermute | solution.py:148
  178.3 23.2 %collective-permute-start.59 = (bf16[2,128,1024]{2,1,0:T(8,128)(2,1)S(1)}, bf16[2,128,1024]{2,1,0:T(8,128)(2,1)S(1)}, u32[]{:S(2)}, u32[]{:S(2)}) collective-permute-start(bf16[2,128,1024]{2,1,0:T(8,128)(2,1)S(1)} %get-tuple-element.118), channel_id=1, source_target_pairs={{0,4},{2,6},{4,0},{6,2},{8,12},{10,14},{12,8},{14,10},{16,20},{18,... | collective-permute-start | bytes 1572872 | tf_op jit(solution)/shard_map/ppermute | solution.py:148
  183.8 22.5 %collective-permute-start.60 = (bf16[2,128,1024]{2,1,0:T(8,128)(2,1)S(1)}, bf16[2,128,1024]{2,1,0:T(8,128)(2,1)S(1)}, u32[]{:S(2)}, u32[]{:S(2)}) collective-permute-start(bf16[2,128,1024]{2,1,0:T(8,128)(2,1)S(1)} %get-tuple-element.119), channel_id=1, source_target_pairs={{0,1},{1,0},{2,3},{3,2},{4,5},{5,4},{6,7},{7,6},{8,9},{9,8},{10,11... | collective-permute-start | bytes 1572872 | tf_op jit(solution)/shard_map/ppermute | solution.py:148
  191.6 23.6 %collective-permute-start.29 = (bf16[128,1024]{1,0:T(8,128)(2,1)S(1)}, bf16[128,1024]{1,0:T(8,128)(2,1)S(1)}, u32[]{:S(2)}, u32[]{:S(2)}) collective-permute-start(bf16[128,1024]{1,0:T(8,128)(2,1)S(1)} %get-tuple-element.90), channel_id=1, source_target_pairs={{0,1},{1,0},{2,3},{3,2},{4,5},{5,4},{6,7},{7,6},{8,9},{9,8},{10,11... | collective-permute-start | bytes 786440 | tf_op jit(solution)/shard_map/ppermute | solution.py:148
  222.2 15.8 %collective-permute-start.63 = (bf16[2,128,1024]{2,1,0:T(8,128)(2,1)S(1)}, bf16[2,128,1024]{2,1,0:T(8,128)(2,1)S(1)}, u32[]{:S(2)}, u32[]{:S(2)}) collective-permute-start(bf16[2,128,1024]{2,1,0:T(8,128)(2,1)S(1)} %get-tuple-element.123), channel_id=1, source_target_pairs={{0,8},{2,10},{4,12},{6,14},{8,16},{10,18},{12,20},{14,22},{16,24},... | collective-permute-start | bytes 1572872 | tf_op jit(solution)/shard_map/ppermute | solution.py:153
  (67 other events, 793.7 us)
